TPU v7x, 32 devices: a whole 2x2x4 slice. The times are simulated.
32 devices in a mesh: dp: 8 (over z, core), shard: 4 (over y, x).
Axes of the slice: x: 2, y: 2, z: 4, core: 2. Of those that a mesh axis runs over, the one named last changes fastest.
Arguments:
- momentum: bfloat16 [8, 2, 4096, 1536], P('dp', None, 'shard'), may hold values from -6 to 6
- right_basis: bfloat16 [8, 2, 128, 1536], P('dp'), as said below
- reach_map: int32 [8, 64], replicated, may hold values from 0 to 1, as said below
Outputs:
- momentum_next: bfloat16 [8, 2, 4096, 1536], P('dp', None, 'shard')
- basis_next: bfloat16 [8, 2, 128, 1536], P('dp')
- left_factor: bfloat16 [8, 2, 4096, 128], P('dp', None, 'shard')
Inputs may be any that keep to these rules, and one draw needn't show every extreme that they name: `reach_map`: each row holds exactly 2 ones; the ones of a row lie in different blocks of 16 consecutive experts; in every draw one block holds a one of every row. Slots of any replicas that hold the same expert hold equal right_basis.
All inputs are finite; a program needn't handle non-finite values.
Results may differ from a plain program's by a relative error of at most 0.018.
Values may be sent and summed in bfloat16 or wider, within the bound.
A program may use at most 64 MiB of HBM per device.

v0:
```python
import math

import jax
import jax.numpy as jnp
from jax import lax
from jax.sharding import PartitionSpec as P

NGROUP = 4


decay_keep = 0.9


def from_partner(value, axis, stride):
    mask = 2**stride
    pairs = [(source, source ^ mask) for source in range(lax.axis_size(axis))]
    return lax.ppermute(value, axis, pairs)


def slot_table(reach_map, slot_count):
    counts = jnp.cumsum(reach_map, axis=1)
    chosen = [((reach_map == 1) & (counts == k + 1)).astype(jnp.int32) for k in range(slot_count)]
    return jnp.stack(chosen, axis=1)


def on_device(momentum, right_basis, reach_map):
    slot_count = momentum.shape[1]
    rows_dev = momentum.shape[2]
    col_count = momentum.shape[3]
    rank_size = right_basis.shape[2]
    experts = reach_map.shape[1]
    groups = NGROUP
    replicas = lax.axis_size("dp")
    group_size = replicas // groups
    rows_own = rows_dev // group_size
    per_group = experts // groups
    per_shard = per_group // lax.axis_size("shard")
    shard_pos = lax.axis_index("shard")
    device = lax.axis_index("dp")
    owner_group = device // group_size
    total_rows = rows_dev * lax.axis_size("shard")
    slot_hits = slot_table(reach_map, slot_count)
    expert_group = lax.broadcasted_iota(jnp.int32, (experts,), 0) // per_group
    group_ids = lax.broadcasted_iota(jnp.int32, (groups,), 0)
    my_slots = lax.dynamic_index_in_dim(slot_hits, device, 0, keepdims=False)
    slot_group = jnp.sum(my_slots * expert_group[None, :], axis=1)
    slot_onehot = (slot_group[:, None] == group_ids[None, :]).astype(jnp.bfloat16)
    partial_value = jnp.einsum(
        "src,skc->srk", momentum[0], right_basis[0], preferred_element_type=jnp.float32
    )
    partial_value = (partial_value * (1.0 / math.sqrt(col_count))).astype(jnp.bfloat16)
    pieces = partial_value.reshape(slot_count, group_size, rows_own, rank_size)
    outgoing = jnp.einsum(
        "sg,sqxk->gqxk", slot_onehot, pieces, preferred_element_type=jnp.float32
    ).astype(jnp.bfloat16)
    outgoing = outgoing.reshape(replicas, rows_own, rank_size)
    incoming = lax.all_to_all(outgoing, "dp", split_axis=0, concat_axis=0, tiled=True)
    owned_hits = lax.dynamic_slice_in_dim(slot_hits, owner_group * per_group, per_group, 2)
    source_owned = jnp.sum(owned_hits, axis=1)
    own_count = jnp.sum(source_owned, axis=0)
    my_count = lax.dynamic_slice_in_dim(own_count, shard_pos * per_shard, per_shard, 0)
    source_weight = source_owned.astype(jnp.bfloat16)
    left_sum = jnp.einsum(
        "rj,rxk->jxk", source_weight, incoming, preferred_element_type=jnp.float32
    )
    gram_local = jnp.einsum("jxa,jxb->jab", left_sum, left_sum, precision=lax.Precision.HIGHEST)
    bit_count = group_size.bit_length() - 1
    gram_sum = lax.psum(gram_local.astype(jnp.bfloat16), "shard").astype(jnp.float32)
    for level in range(bit_count):
        gram_sum = gram_sum + from_partner(gram_sum.astype(jnp.bfloat16), "dp", level).astype(
            gram_sum.dtype
        )
    my_gram = lax.dynamic_slice_in_dim(gram_sum, shard_pos * per_shard, per_shard, 0)
    identity = jnp.eye(rank_size, dtype=jnp.float32)
    my_gram = my_gram + identity[None] * (my_count == 0).astype(jnp.float32)[:, None, None]
    factor = jnp.linalg.cholesky(my_gram)
    my_inverse = jax.vmap(lambda m: jax.scipy.linalg.solve_triangular(m, identity, lower=True))(
        factor
    )
    inverse = lax.all_gather(my_inverse.astype(jnp.bfloat16), "shard", axis=0, tiled=True).astype(
        my_inverse.dtype
    )
    scaled = inverse * math.sqrt(total_rows)
    ortho_rows = jnp.einsum(
        "jxk,jyk->jxy", left_sum, scaled, precision=lax.Precision.HIGHEST
    ).astype(jnp.bfloat16)
    send_back = jnp.einsum(
        "rj,jxy->rxy", source_weight, ortho_rows, preferred_element_type=jnp.float32
    ).astype(jnp.bfloat16)
    arrived = lax.all_to_all(send_back, "dp", split_axis=0, concat_axis=0, tiled=True)
    arrived = arrived.reshape(groups, group_size, rows_own, rank_size)
    left_factor = jnp.einsum(
        "sg,gqxk->sqxk", slot_onehot, arrived, preferred_element_type=jnp.float32
    ).astype(jnp.bfloat16)
    left_factor = left_factor.reshape(slot_count, rows_dev, rank_size)
    right_part = jnp.einsum(
        "srk,src->skc", left_factor, momentum[0], preferred_element_type=jnp.float32
    )
    right_part = (right_part * (1.0 / math.sqrt(total_rows))).astype(jnp.bfloat16)
    right_share = (
        lax.psum_scatter(right_part, "shard", scatter_dimension=1, tiled=True)
        .astype(jnp.float32)
        .astype(jnp.bfloat16)
    )
    right_full = lax.all_gather(right_share, "shard", axis=1, tiled=True)
    right_wide = right_full.astype(jnp.float32)
    basis_next = (
        right_wide * lax.rsqrt(jnp.mean(right_wide * right_wide, axis=2, keepdims=True) + 1e-06)
    ).astype(jnp.bfloat16)
    update = jnp.einsum("sxk,skc->sxc", left_factor, right_full, preferred_element_type=jnp.float32)
    momentum_next = (
        momentum[0].astype(jnp.float32) - (1.0 - decay_keep) / math.sqrt(total_rows) * update
    ).astype(jnp.bfloat16)
    return (momentum_next[None], basis_next[None], left_factor[None])


def solution(mesh):
    return jax.shard_map(
        on_device,
        mesh=mesh,
        in_specs=(P("dp", None, "shard", None), P("dp", None, None, None), P()),
        out_specs=(
            P("dp", None, "shard", None),
            P("dp", None, None, None),
            P("dp", None, "shard", None),
        ),
        check_vma=False,
    )
```

profile of v0, /device:TPU:24, one launch (start us, length us, event | category | flops | bytes accessed | tf_op | source)
XLA Modules:
  0.0 297.6 jit_solution(7352647711727268570)
XLA Ops:
  7.2 1.0 reduce_window_sum.11
  8.9 4.6 %fusion.28 = bf16[2,1024,128]{2,1,0:T(8,128)(2,1)S(1)} fusion(bf16[1,2,1024,1536]{3,2,1,0:T(8,128)(2,1)} %param.3, bf16[1,2,128,1536]{3,2,1,0:T(8,128)(2,1)S(1)} %copy-done), kind=kOutput, calls=%fused_computation.22 | convolution fusion | flops 805830656 | bytes 7602176 | tf_op jit(solution)/shard_map/src,skc->srk/dot_general | solution.py:48
  13.6 1.2 convolution_convert_fusion
  14.8 1.1 copy.62
  15.9 5.1 %all-to-all-start = ((bf16[8,512,128]{2,1,0:T(8,128)(2,1)}), bf16[8,512,128]{2,1,0:T(8,128)(2,1)S(1)}, u32[]{:S(2)}, u32[]{:S(2)}) async-start(bf16[8,512,128]{2,1,0:T(8,128)(2,1)} %bitcast.10), calls=%async_computation | async-start | bytes 2097152 | tf_op jit(solution)/shard_map/all_to_all | solution.py:57
  21.1 23.9 %all-to-all-done = bf16[8,512,128]{2,1,0:T(8,128)(2,1)S(1)} async-done(((bf16[8,512,128]{2,1,0:T(8,128)(2,1)}), bf16[8,512,128]{2,1,0:T(8,128)(2,1)S(1)}, u32[]{:S(2)}, u32[]{:S(2)}) %all-to-all-start) | async-done | bytes 1048608 | tf_op jit(solution)/shard_map/all_to_all | solution.py:57
  45.9 2.0 copy-done.1
  47.9 10.2 %fusion.31 = bf16[16,128,128]{1,2,0:T(8,128)(2,1)} fusion(f32[16,512,128]{2,0,1:T(8,128)S(1)} %fusion.34), kind=kOutput, calls=%fused_computation.23 | convolution fusion | flops 1610874880 | bytes 4718592 | tf_op jit(solution)/shard_map/jxa,jxb->jab/dot_general | solution.py:66
  58.4 46.2 %all-reduce.2.cloned.1.call-done = bf16[16,128,128]{1,2,0:T(8,128)(2,1)} async-done(((bf16[16,128,128]{1,2,0:T(8,128)(2,1)}), bf16[16,128,128]{1,2,0:T(8,128)(2,1)}) %all-reduce.2.cloned.1.call-update) | async-done | bytes 524304 | tf_op jit(solution)/shard_map/psum | solution.py:68
  104.9 1.9 collective-permute-done
  106.8 1.0 multiply_add_fusion
  108.0 46.9 %custom-call.8 = f32[4,128,128]{2,1,0:T(8,128)S(1)} custom-call(f32[4,128,128]{2,1,0:T(8,128)S(1)} %fusion.46), custom_call_target="Cholesky" | custom-call | tf_op jit(solution)/shard_map/jit(cholesky)/cholesky | solution.py:76
  155.1 39.3 %custom-call.9 = f32[4,1,128,128]{2,3,1,0:T(8,128)S(1)} custom-call(f32[4,1,128,128]{3,2,1,0:T(8,128)S(1)} %select_bitcast_fusion), custom_call_target="InvertDiagBlocksLowerTriangular" | custom-call | tf_op jit(solution)/shard_map/vmap(jit(_solve_triangular))/triangular_solve | solution.py:77
  195.1 10.0 %all_gather.6 = bf16[16,128,128]{2,1,0:T(8,128)(2,1)S(1)} all-gather(bf16[4,128,128]{2,1,0:T(8,128)(2,1)S(1)} %convolution_convert_fusion.2), channel_id=1, replica_groups=mesh['dp'=8,'shard'=4] {'shard'}, dimensions={0}, use_global_device_ids=true | all-gather | bytes 655360 | tf_op jit(solution)/shard_map/all_gather | solution.py:80
  205.1 6.5 %fusion.17 = bf16[16,512,128]{2,1,0:T(8,128)(2,1)S(1)} fusion(f32[16,512,128]{2,0,1:T(8,128)} %copy-done.1, bf16[16,128,128]{2,1,0:T(8,128)(2,1)S(1)} %all_gather.6), kind=kOutput, calls=%fused_computation.16 | convolution fusion | flops 1612185600 | bytes 6815744 | tf_op jit(solution)/shard_map/jxk,jyk->jxy/dot_general | solution.py:84
  211.6 1.3 fusion.22
  213.0 28.9 %all_to_all.10 = bf16[8,512,128]{2,1,0:T(8,128)(2,1)S(1)} all-to-all(bf16[8,512,128]{2,1,0:T(8,128)(2,1)S(1)} %copy.73), channel_id=1, replica_groups=mesh['dp'=8,'shard'=4] {'dp'}, dimensions={0} | all-to-all | bytes 2097152 | tf_op jit(solution)/shard_map/all_to_all | solution.py:90
  241.9 1.0 convolution_convert_fusion.1
  242.9 1.9 fusion.12
  244.8 0.9 copy.77
  245.7 25.4 %reduce-scatter.2.cloned.1.call-done = bf16[2,32,1536]{2,1,0:T(8,128)(2,1)} async-done(((bf16[2,128,1536]{2,1,0:T(8,128)(2,1)}), bf16[2,32,1536]{2,1,0:T(8,128)(2,1)}) %reduce-scatter.2.cloned.1.call-update) | async-done | bytes 196624 | tf_op jit(solution)/shard_map/reduce_scatter | solution.py:101
  271.1 11.1 %all_gather.7 = bf16[2,128,1536]{2,1,0:T(8,128)(2,1)S(1)} all-gather(bf16[2,32,1536]{2,1,0:T(8,128)(2,1)} %reduce-scatter.2.cloned.1.call-done), channel_id=1, replica_groups=mesh['dp'=8,'shard'=4] {'shard'}, dimensions={1}, use_global_device_ids=true | all-gather | bytes 983040 | tf_op jit(solution)/shard_map/all_gather | solution.py:105
  282.2 7.3 %fusion.4 = bf16[1,2,1024,1536]{3,2,1,0:T(8,128)(2,1)} fusion(bf16[2,128,1536]{2,1,0:T(8,128)(2,1)S(1)} %all_gather.7, bf16[1,2,1024,1536]{3,2,1,0:T(8,128)(2,1)} %param.3, bf16[2,1024,128]{2,0,1:T(2,128)(2,1)S(1)} %bitcast.59), kind=kOutput, calls=%fused_computation.5 | convolution fusion | flops 817889280 | bytes 13893632 | tf_op jit(solution)/shard_map/sxk,skc->sxc/dot_general | solution.py:110
  289.7 1.1 fusion.39
  (35 shorter events, 3.7 us)
Async XLA Ops:
  7.2 1.7 copy-start
  15.9 29.1 %all-to-all-start = ((bf16[8,512,128]{2,1,0:T(8,128)(2,1)}), bf16[8,512,128]{2,1,0:T(8,128)(2,1)S(1)}, u32[]{:S(2)}, u32[]{:S(2)}) async-start(bf16[8,512,128]{2,1,0:T(8,128)(2,1)} %bitcast.10), calls=%async_computation | async-start | bytes 2097152 | tf_op jit(solution)/shard_map/all_to_all | solution.py:57
  21.0 83.6 %all-reduce.2.cloned.1.call-start = ((), (), s32[]{:S(2)}) async-start(), calls=%async_computation.3 | async-start | bytes 1048576 | tf_op jit(solution)/shard_map/psum | solution.py:68
  45.9 2.0 copy-start.1
  58.2 212.9 %reduce-scatter.2.cloned.1.call-start = ((), (), s32[]{:S(2)}) async-start(), calls=%async_computation.4 | async-start | bytes 983040 | tf_op jit(solution)/shard_map/reduce_scatter | solution.py:101
  104.7 2.1 collective-permute-start
  205.1 37.8 %slice-start = ((s8[6291456]{0:T(1024)(128)(4,1)}), s8[4194304]{0:T(1024)(128)(4,1)S(1)}, s32[]{:S(2)}) async-start(s8[6291456]{0:T(1024)(128)(4,1)} %bitcast.55), calls=%async_computation.5 | async-start | bytes 8388608
  211.6 31.3 %slice-start.1 = ((s8[6291456]{0:T(1024)(128)(4,1)}), s8[2097152]{0:T(1024)(128)(4,1)S(1)}, s32[]{:S(2)}) async-start(s8[6291456]{0:T(1024)(128)(4,1)} %bitcast.55), calls=%async_computation.6 | async-start | bytes 4194304
Sparse Core Ops, SparseCore 0:
  58.3 46.3 all-reduce.1
  245.0 26.0 reduce-scatter.1
where the time goes:
time: 300 us; the launch traced here: 298 us
  waiting for transfers between devices  97.5 us (32%)
  other arithmetic  90.8 us (30%)
  blocking collectives  50 us (17%)
  matrix products  35.3 us (12%)
  between operations  14.2 us (5%)
  starting transfers between devices  5.33 us (2%)
  local copies, waits for them, and re-layouts  4.4 us (1%)
    another operation x4, other arithmetic, on_device(): factor = jnp.linalg.cholesky(my_gram)  47.1 us
    psum x1, waiting for transfers between devices, on_device(): lax.psum(gram_local.astype(jnp.bfloat16), 'shard').astype(jnp.float32)  46.2 us
    another operation x3, other arithmetic, on_device(): jax.scipy.linalg.solve_triangular(m, identity, lower=True)  39.4 us
    all_to_all x1, blocking collectives, on_device(): lax.all_to_all(send_back, 'dp', split_axis=0, concat_axis=0, tiled=True)  28.9 us
    reduce_scatter x1, waiting for transfers between devices, on_device(): lax.psum_scatter(right_part, 'shard', scatter_dimension=1, tiled=True)  25.4 us
    all_to_all x1, waiting for transfers between devices, on_device(): lax.all_to_all(outgoing, 'dp', split_axis=0, concat_axis=0, tiled=True)  23.9 us
    all_gather x1, blocking collectives, on_device(): right_full = lax.all_gather(right_share, 'shard', axis=1, tiled=True)  11.1 us
    dot_general x1, matrix products, on_device(): jnp.einsum('jxa,jxb->jab', left_sum, left_sum, precision=lax.Precision.HI...  10.2 us
  transfers between devices with their start and end apart: 4, of which 4 were waited for; matrix products, arithmetic and copies ran while one was open for 0% of the time, Pallas kernels for 0%

commit v1 on v0

--- a/solution.py
+++ b/solution.py
@@ -1,8 +1,11 @@
+import functools
 import math
 
 import jax
 import jax.numpy as jnp
 from jax import lax
+from jax.experimental import pallas as pl
+from jax.experimental.pallas import tpu as pltpu
 from jax.sharding import PartitionSpec as P
 
 NGROUP = 4
@@ -114,9 +117,471 @@
     return (momentum_next[None], basis_next[None], left_factor[None])
 
 
+MESH = pl.DeviceIdType.MESH
+ROUND = 8
+EARLY_ROUNDS = 5
+
+
+def remote(src, dst, send_sem, recv_sem, device):
+    return pltpu.make_async_remote_copy(
+        src_ref=src,
+        dst_ref=dst,
+        send_sem=send_sem,
+        recv_sem=recv_sem,
+        device_id=device,
+        device_id_type=MESH,
+    )
+
+
+def dot_nt(a, b):
+    return lax.dot_general(a, b, (((1,), (1,)), ((), ())), preferred_element_type=jnp.float32)
+
+
+def dot_tn(a, b):
+    return lax.dot_general(a, b, (((0,), (0,)), ((), ())), preferred_element_type=jnp.float32)
+
+
+def slot_classes(reach, groups):
+    lane = lax.broadcasted_iota(jnp.int32, reach.shape, 1)
+    width = reach.shape[1] // groups
+    hot_lanes = jnp.zeros(reach.shape, jnp.float32)
+    taken = jnp.zeros((1, 1), jnp.float32)
+    for group in range(groups):
+        inside = ((lane >= group * width) & (lane < (group + 1) * width)).astype(jnp.float32)
+        row_count = jnp.sum(reach * inside, axis=1, keepdims=True)
+        full = jnp.min(row_count, axis=0, keepdims=True)
+        pick = jnp.where(full > 0.5, 1.0, 0.0) * (1.0 - taken)
+        taken = taken + pick
+        hot_lanes = hot_lanes + pick * inside
+    lane_id = lane.astype(jnp.float32)
+    hot = jnp.sum(reach * hot_lanes * lane_id, axis=1, keepdims=True)
+    cold = jnp.sum(reach * (1.0 - hot_lanes) * lane_id, axis=1, keepdims=True)
+    return hot, cold
+
+
+def eliminate_round(step, mat):
+    rank = mat.shape[1]
+    row_id = lax.broadcasted_iota(jnp.int32, mat.shape, 1)
+    lane_id = lax.broadcasted_iota(jnp.int32, mat.shape, 2)
+    left = rank - ROUND * step
+    for m in range(ROUND):
+        row = mat[:, m : m + 1, :]
+        pivot = 1.0 / row[:, :, m : m + 1]
+        active = (row_id > m) & (row_id < left)
+        ratio = jnp.where(active, mat[:, :, m : m + 1] * pivot, 0.0)
+        row_one = jnp.where(lane_id[:, :1] == m, 1.0, row)
+        mat = jnp.where(active & (lane_id == m), 0.0, mat) - ratio * row_one
+    mat = jnp.concatenate([mat[:, ROUND:], mat[:, :ROUND]], axis=1)
+    return pltpu.roll(mat, rank - ROUND, axis=2)
+
+
+def power_kernel(
+    groups,
+    m_hbm,
+    b_hbm,
+    reach_ref,
+    q_ref,
+    inv_ref,
+    r_ref,
+    m_buf,
+    b_buf,
+    p_out,
+    p_in,
+    q_out,
+    q_in,
+    g_out,
+    g_in,
+    x_out,
+    x_in,
+    t_out,
+    t_in,
+    t_red,
+    t_full,
+    m_sem,
+    b_sem,
+    p_send,
+    p_recv,
+    q_send,
+    q_recv,
+    g_send,
+    g_recv,
+    x_send,
+    x_recv,
+    t_send,
+    t_recv,
+    f_send,
+    f_recv,
+):
+    me = lax.axis_index("dp")
+    sp = lax.axis_index("shard")
+    replicas = p_in.shape[0]
+    pieces = replicas // 2
+    rows = p_in.shape[1]
+    shards = t_full.shape[0]
+    wide = t_full.shape[3]
+    cols = m_buf.shape[2]
+    rank = b_buf.shape[1]
+    core = lax.rem(me, 2)
+    zed = me // 2
+    order = list(range(pieces // 2, pieces)) + list(range(1, pieces // 2)) + [0]
+
+    def piece_at(o):
+        return lax.rem(zed + o, pieces)
+
+    def span(q):
+        return pl.ds(pl.multiple_of(q * rows, rows), rows)
+
+    for k in range(2):
+        pltpu.make_async_copy(b_hbm.at[k], b_buf.at[k], b_sem.at[k]).start()
+    for o in order:
+        for k in range(2):
+            at = span(piece_at(o))
+            pltpu.make_async_copy(m_hbm.at[k, at], m_buf.at[k, at], m_sem.at[o, k]).start()
+
+    barrier = pltpu.get_barrier_semaphore()
+    for o in range(1, replicas):
+        pl.semaphore_signal(barrier, 1, device_id=(lax.rem(me + o, replicas), sp), device_id_type=MESH)
+    for o in range(1, shards):
+        for cc in range(2):
+            pl.semaphore_signal(
+                barrier, 1, device_id=(2 * zed + cc, lax.rem(sp + o, shards)), device_id_type=MESH
+            )
+
+    hot, cold = slot_classes(reach_ref[...].astype(jnp.float32), groups)
+    mine = lax.broadcasted_iota(jnp.int32, (replicas, 1), 0) == me
+    my_hot = jnp.sum(jnp.where(mine, hot, 0.0), axis=0, keepdims=True)
+    my_cold = jnp.sum(jnp.where(mine, cold, 0.0), axis=0, keepdims=True)
+    first = jnp.where(my_hot < my_cold, 1.0, 0.0)
+    ids = jnp.where(core == 0, hot, cold)
+    diag = lax.broadcasted_iota(jnp.int32, (replicas, replicas), 0) == lax.broadcasted_iota(
+        jnp.int32, (replicas, replicas), 1
+    )
+    ids_row = jnp.sum(jnp.where(diag, ids, 0.0), axis=0, keepdims=True)
+    same = jnp.where(ids == ids_row, 1.0, 0.0)
+
+    for k in range(2):
+        pltpu.make_async_copy(b_hbm.at[k], b_buf.at[k], b_sem.at[k]).wait()
+
+    for n, o in enumerate(order):
+        q = piece_at(o)
+        at = span(q)
+        part = []
+        for k in range(2):
+            pltpu.make_async_copy(m_hbm.at[k, at], m_buf.at[k, at], m_sem.at[o, k]).wait()
+            value = dot_nt(m_buf[k, at, :], b_buf[k]) * (1.0 / math.sqrt(cols))
+            part.append(value)
+        p_out[o, 0] = (part[0] * first + part[1] * (1.0 - first)).astype(jnp.bfloat16)
+        p_out[o, 1] = (part[1] * first + part[0] * (1.0 - first)).astype(jnp.bfloat16)
+        if n == 0:
+            pl.semaphore_wait(barrier, replicas - 1 + 2 * (shards - 1))
+        if o > 0:
+            for cc in range(2):
+                remote(
+                    p_out.at[o, cc], p_in.at[me], p_send.at[o, cc], p_recv.at[me], (2 * q + cc, sp)
+                ).start()
+        else:
+            other = 1 - core
+            remote(
+                p_out.at[0, other], p_in.at[me], p_send.at[0, 0], p_recv.at[me], (2 * q + other, sp)
+            ).start()
+            p_in[me] = p_out[0, core]
+
+    for o in range(1, replicas):
+        src = lax.rem(me + o, replicas)
+        remote(p_out.at[0, 0], p_in.at[src], p_send.at[0, 0], p_recv.at[src], (src, sp)).wait_recv()
+
+    for zz in range(pieces):
+        for cc in range(2):
+            i = 2 * zz + cc
+            total = jnp.zeros((rows, rank), jnp.float32)
+            for j in range(replicas):
+                total = total + same[i : i + 1, j : j + 1] * p_in[j].astype(jnp.float32)
+            rounded = total.astype(jnp.bfloat16)
+            q_out[i] = rounded
+            g_out[zz, cc] = dot_tn(rounded, rounded).astype(jnp.bfloat16)
+
+        @pl.when(zz != zed)
+        def _():
+            remote(
+                g_out.at[zz], g_in.at[zed], g_send.at[zz], g_recv.at[zed], (2 * zz + core, sp)
+            ).start()
+
+        @pl.when(zz == zed)
+        def _():
+            g_in[zz] = g_out[zz]
+
+    for o in range(1, replicas):
+        dst = lax.rem(me + o, replicas)
+        remote(
+            q_out.at[dst],
+            q_in.at[core, span(zed)],
+            q_send.at[o],
+            q_recv.at[core, zed],
+            (dst, sp),
+        ).start()
+    q_in[core, span(zed), :] = q_out[me]
+
+    for o in range(1, pieces):
+        src = piece_at(o)
+        remote(
+            g_out.at[0], g_in.at[src], g_send.at[0], g_recv.at[src], (2 * src + core, sp)
+        ).wait_recv()
+    for cc in range(2):
+        gram = g_in[0, cc].astype(jnp.float32)
+        for zz in range(1, pieces):
+            gram = gram + g_in[zz, cc].astype(jnp.float32)
+        x_out[cc] = gram.astype(jnp.bfloat16)
+    peers = [(dc, o) for o in range(shards) for dc in range(2) if (dc, o) != (0, 0)]
+    for dc, o in peers:
+        cc = lax.rem(core + dc, 2)
+        sq = lax.rem(sp + o, shards)
+        remote(
+            x_out.at[cc], x_in.at[core, sp], x_send.at[dc, o], x_recv.at[core, sp], (2 * zed + cc, sq)
+        ).start()
+    x_in[core, sp] = x_out[core]
+    for dc, o in peers:
+        cc = lax.rem(core + dc, 2)
+        sq = lax.rem(sp + o, shards)
+        remote(
+            x_out.at[0], x_in.at[cc, sq], x_send.at[dc, o], x_recv.at[cc, sq], (2 * zed + cc, sq)
+        ).wait_recv()
+
+    square = (rank, rank)
+    eye_mask = lax.broadcasted_iota(jnp.int32, square, 0) == lax.broadcasted_iota(
+        jnp.int32, square, 1
+    )
+    identity = jnp.where(eye_mask, 1.0, 0.0)
+    grams = []
+    for c, (table, own) in enumerate(((hot, my_hot), (cold, my_cold))):
+        count = jnp.sum(jnp.where(table == own, 1.0, 0.0), axis=0, keepdims=True)
+        gram = x_in[c, 0].astype(jnp.float32)
+        for sq in range(1, shards):
+            gram = gram + x_in[c, sq].astype(jnp.float32)
+        grams.append(gram + identity * jnp.where(count < 0.5, 1.0, 0.0))
+    mat = jnp.stack(grams, axis=0)
+    rounds = rank // ROUND
+    mat = lax.fori_loop(0, EARLY_ROUNDS, eliminate_round, mat)
+
+    for cc in range(2):
+        for zz in range(pieces):
+
+            @pl.when((cc != core) | (zz != zed))
+            def _():
+                remote(
+                    q_out.at[0],
+                    q_in.at[cc, pl.ds(zz * rows, rows)],
+                    q_send.at[0],
+                    q_recv.at[cc, zz],
+                    (2 * zz + cc, sp),
+                ).wait_recv()
+
+    for zz in range(pieces):
+        at = pl.ds(zz * rows, rows)
+        a = q_in[0, at, :].astype(jnp.float32)
+        b = q_in[1, at, :].astype(jnp.float32)
+        q_ref[0, at, :] = (a * first + b * (1.0 - first)).astype(jnp.bfloat16)
+        q_ref[1, at, :] = (b * first + a * (1.0 - first)).astype(jnp.bfloat16)
+    turned = [q_ref[k].T for k in range(2)]
+    for o in list(range(1, shards)) + [0]:
+        sq = lax.rem(sp + o, shards)
+        at = pl.ds(pl.multiple_of(sq * wide, wide), wide)
+        for k in range(2):
+            value = jnp.dot(turned[k], m_buf[k, :, at], preferred_element_type=jnp.float32)
+            t_out[o, k] = value.astype(jnp.bfloat16)
+        if o > 0:
+            remote(t_out.at[o], t_in.at[sp], t_send.at[o], t_recv.at[sp], (me, sq)).start()
+        else:
+            t_in[sp] = t_out[0]
+
+    mat = lax.fori_loop(EARLY_ROUNDS, rounds, eliminate_round, mat)
+
+    for o in range(1, shards):
+        sq = lax.rem(sp + o, shards)
+        remote(t_out.at[0], t_in.at[sq], t_send.at[0], t_recv.at[sq], (me, sq)).wait_recv()
+    for k in range(2):
+        value = t_in[0, k].astype(jnp.float32)
+        for sq in range(1, shards):
+            value = value + t_in[sq, k].astype(jnp.float32)
+        t_red[k] = value.astype(jnp.bfloat16)
+    for o in range(1, shards):
+        sq = lax.rem(sp + o, shards)
+        remote(t_red, t_full.at[sp], f_send.at[o], f_recv.at[sp], (me, sq)).start()
+    t_full[sp] = t_red[...]
+
+    below = lax.broadcasted_iota(jnp.int32, square, 0) > lax.broadcasted_iota(jnp.int32, square, 1)
+    inverse = []
+    for c in range(2):
+        pivots = jnp.sum(jnp.where(eye_mask, mat[c], 0.0), axis=1, keepdims=True)
+        unit = jnp.where(below, mat[c], identity)
+        inverse.append(unit * lax.rsqrt(pivots))
+    ordered = [
+        (inverse[0] * first + inverse[1] * (1.0 - first)).astype(jnp.bfloat16),
+        (inverse[1] * first + inverse[0] * (1.0 - first)).astype(jnp.bfloat16),
+    ]
+    for k in range(2):
+        inv_ref[k] = ordered[k]
+
+    for o in range(1, shards):
+        sq = lax.rem(sp + o, shards)
+        remote(t_red, t_full.at[sq], f_send.at[o], f_recv.at[sq], (me, sq)).wait_recv()
+    for sq in range(shards):
+        for k in range(2):
+            value = jnp.dot(ordered[k], t_full[sq, k], preferred_element_type=jnp.float32)
+            r_ref[k, :, sq * wide : (sq + 1) * wide] = value.astype(jnp.bfloat16)
+
+    for o in order:
+        for cc in range(2 if o > 0 else 1):
+            remote(
+                p_out.at[o, cc], p_in.at[me], p_send.at[o, cc], p_recv.at[me], (2 * zed + 1 - core, sp)
+            ).wait_send()
+    for o in range(1, replicas):
+        dst = lax.rem(me + o, replicas)
+        remote(
+            q_out.at[dst], q_in.at[core, span(zed)], q_send.at[o], q_recv.at[core, zed], (dst, sp)
+        ).wait_send()
+    for zz in range(pieces):
+
+        @pl.when(zz != zed)
+        def _():
+            remote(
+                g_out.at[zz], g_in.at[zed], g_send.at[zz], g_recv.at[zed], (2 * zz + core, sp)
+            ).wait_send()
+
+    for dc, o in peers:
+        cc = lax.rem(core + dc, 2)
+        sq = lax.rem(sp + o, shards)
+        remote(
+            x_out.at[cc], x_in.at[core, sp], x_send.at[dc, o], x_recv.at[core, sp], (2 * zed + cc, sq)
+        ).wait_send()
+    for o in range(1, shards):
+        sq = lax.rem(sp + o, shards)
+        remote(t_out.at[o], t_in.at[sp], t_send.at[o], t_recv.at[sp], (me, sq)).wait_send()
+        remote(t_red, t_full.at[sp], f_send.at[o], f_recv.at[sp], (me, sq)).wait_send()
+
+
+def finish_kernel(total_rows, m_ref, q_ref, inv_ref, r_ref, out_ref, basis_ref, left_ref):
+    r_value = r_ref[0]
+    scale = math.sqrt(total_rows)
+    left = (dot_nt(q_ref[0], inv_ref[0]) * scale).astype(jnp.bfloat16)
+    left_ref[0] = left
+    update = jnp.dot(left, r_value, preferred_element_type=jnp.float32)
+    out_ref[0] = (m_ref[0].astype(jnp.float32) - ((1.0 - decay_keep) / scale) * update).astype(
+        jnp.bfloat16
+    )
+
+    @pl.when(pl.program_id(1) == 0)
+    def _():
+        r_wide = r_value.astype(jnp.float32)
+        mean = jnp.mean(r_wide * r_wide, axis=1, keepdims=True)
+        basis_ref[0] = (r_wide * lax.rsqrt(mean + 1e-06)).astype(jnp.bfloat16)
+
+
+def fused_on_device(momentum, right_basis, reach_map):
+    momentum = momentum[0]
+    right_basis = right_basis[0]
+    slots, rows_dev, cols = momentum.shape
+    rank = right_basis.shape[1]
+    replicas = lax.axis_size("dp")
+    shards = lax.axis_size("shard")
+    pieces = replicas // 2
+    rows = rows_dev // pieces
+    wide = cols // shards
+    bf16 = jnp.bfloat16
+    dma = pltpu.SemaphoreType.DMA
+    vmem = pl.BlockSpec(memory_space=pltpu.VMEM)
+    hbm = pl.BlockSpec(memory_space=pl.ANY)
+    q, inv, r = pl.pallas_call(
+        functools.partial(power_kernel, NGROUP),
+        out_shape=(
+            jax.ShapeDtypeStruct((2, rows_dev, rank), bf16),
+            jax.ShapeDtypeStruct((2, rank, rank), bf16),
+            jax.ShapeDtypeStruct((2, rank, cols), bf16),
+        ),
+        in_specs=[hbm, hbm, vmem],
+        out_specs=(vmem, vmem, vmem),
+        scratch_shapes=[
+            pltpu.VMEM((2, rows_dev, cols), bf16),
+            pltpu.VMEM((2, rank, cols), bf16),
+            pltpu.VMEM((pieces, 2, rows, rank), bf16),
+            pltpu.VMEM((replicas, rows, rank), bf16),
+            pltpu.VMEM((replicas, rows, rank), bf16),
+            pltpu.VMEM((2, rows_dev, rank), bf16),
+            pltpu.VMEM((pieces, 2, rank, rank), bf16),
+            pltpu.VMEM((pieces, 2, rank, rank), bf16),
+            pltpu.VMEM((2, rank, rank), bf16),
+            pltpu.VMEM((2, shards, rank, rank), bf16),
+            pltpu.VMEM((shards, 2, rank, wide), bf16),
+            pltpu.VMEM((shards, 2, rank, wide), bf16),
+            pltpu.VMEM((2, rank, wide), bf16),
+            pltpu.VMEM((shards, 2, rank, wide), bf16),
+            dma((pieces, 2)),
+            dma((2,)),
+            dma((pieces, 2)),
+            dma((replicas,)),
+            dma((replicas,)),
+            dma((2, pieces)),
+            dma((pieces,)),
+            dma((pieces,)),
+            dma((2, shards)),
+            dma((2, shards)),
+            dma((shards,)),
+            dma((shards,)),
+            dma((shards,)),
+            dma((shards,)),
+        ],
+        compiler_params=pltpu.CompilerParams(
+            collective_id=0, has_side_effects=True, vmem_limit_bytes=48 * 1024 * 1024
+        ),
+    )(momentum, right_basis, reach_map)
+    block = rows_dev // 2
+    momentum_next, basis_next, left_factor = pl.pallas_call(
+        functools.partial(finish_kernel, rows_dev * shards),
+        grid=(slots, rows_dev // block),
+        out_shape=(
+            jax.ShapeDtypeStruct((2, rows_dev, cols), bf16),
+            jax.ShapeDtypeStruct((2, rank, cols), bf16),
+            jax.ShapeDtypeStruct((2, rows_dev, rank), bf16),
+        ),
+        in_specs=[
+            pl.BlockSpec((1, block, cols), lambda k, i: (k, i, 0)),
+            pl.BlockSpec((1, block, rank), lambda k, i: (k, i, 0)),
+            pl.BlockSpec((1, rank, rank), lambda k, i: (k, 0, 0)),
+            pl.BlockSpec((1, rank, cols), lambda k, i: (k, 0, 0)),
+        ],
+        out_specs=(
+            pl.BlockSpec((1, block, cols), lambda k, i: (k, i, 0)),
+            pl.BlockSpec((1, rank, cols), lambda k, i: (k, 0, 0)),
+            pl.BlockSpec((1, block, rank), lambda k, i: (k, i, 0)),
+        ),
+        compiler_params=pltpu.CompilerParams(vmem_limit_bytes=40 * 1024 * 1024),
+    )(momentum, q, inv, r)
+    return (momentum_next[None], basis_next[None], left_factor[None])
+
+
+def device_program(momentum, right_basis, reach_map):
+    slots, rows_dev, cols = momentum.shape[1:]
+    rank = right_basis.shape[2]
+    replicas = lax.axis_size("dp")
+    shards = lax.axis_size("shard")
+    pieces = max(replicas // 2, 1)
+    fits = (
+        slots == 2
+        and replicas % 2 == 0
+        and pieces > 1
+        and shards > 1
+        and replicas <= 16
+        and rows_dev % (16 * pieces) == 0
+        and cols % (128 * shards) == 0
+        and rank == 128
+    )
+    if fits:
+        return fused_on_device(momentum, right_basis, reach_map)
+    return on_device(momentum, right_basis, reach_map)
+
+
 def solution(mesh):
     return jax.shard_map(
-        on_device,
+        device_program,
         mesh=mesh,
         in_specs=(P("dp", None, "shard", None), P("dp", None, None, None), P()),
         out_specs=(

time: 300 us -> 69.3 us (0.23)
  the two profiles are of different devices: /device:TPU:24 before, /device:TPU:0 now
where the time goes in v1:
time: 69.3 us; the launch traced here: 69.1 us
  Pallas kernels  66.2 us (96%)
  local copies, waits for them, and re-layouts  2.21 us (3%)
    pallas_call x1, Pallas kernels, fused_on_device(): pl.pallas_call(functools.partial(power_kernel, NGROUP), out_shape=(jax.Sh...  61 us
    pallas_call x1, Pallas kernels, fused_on_device(): pl.pallas_call(functools.partial(finish_kernel, rows_dev * shards), grid=...  5.21 us
    unnamed x6, local copies, waits for them, and re-layouts  2.21 us

profile of v1, /device:TPU:0, one launch (start us, length us, event | category | flops | bytes accessed | tf_op | source)
XLA Modules:
  0.0 69.1 jit_solution(862483218529600135)
XLA Ops:
  0.6 0.0 copy-start
  0.6 0.0 copy-start.1
  0.7 1.3 %copy-done.1 = bf16[1,2,128,1536]{3,2,1,0:T(8,128)(2,1)S(1)} copy-done((bf16[1,2,128,1536]{3,2,1,0:T(8,128)(2,1)S(1)}, bf16[1,2,128,1536]{3,2,1,0:T(8,128)(2,1)}, u32[]{:S(2)}) %copy-start.1) | copy-done | bytes 786456
  1.9 0.0 copy-start.2
  1.9 0.9 %copy-done.2 = s32[8,64]{1,0:T(8,128)S(1)} copy-done((s32[8,64]{1,0:T(8,128)S(1)}, s32[8,64]{1,0:T(8,128)}, u32[]{:S(2)}) %copy-start.2) | copy-done | bytes 2072
  2.9 61.0 %shard_map.58 = (bf16[2,1024,128]{2,1,0:T(8,128)(2,1)S(1)}, bf16[2,128,128]{2,1,0:T(8,128)(2,1)S(1)}, bf16[2,128,1536]{2,1,0:T(8,128)(2,1)S(1)}) custom-call(bf16[2,1024,1536]{2,1,0:T(8,128)(2,1)} %bitcast.5, bf16[2,128,1536]{2,1,0:T(8,128)(2,1)S(1)} %bitcast.7, s32[8,64]{1,0:T(8,128)S(1)} %copy-done.2), custom_call_target="tpu_custom_call" | custom-call | tf_op jit(solution)/shard_map/pallas_call | solution.py:493
  63.9 0.0 copy-done
  63.9 5.2 %shard_map.59 = (bf16[2,1024,1536]{2,1,0:T(8,128)(2,1)}, bf16[2,128,1536]{2,1,0:T(8,128)(2,1)}, bf16[2,1024,128]{2,1,0:T(8,128)(2,1)}) custom-call(bf16[2,1024,1536]{2,1,0:T(8,128)(2,1)S(1)} %bitcast.6, bf16[2,1024,128]{2,1,0:T(8,128)(2,1)S(1)} %get-tuple-element.9.q_ref, bf16[2,128,128]{2,1,0:T(8,128)(2,1)S(1)} %get-tuple-element.10.inv_ref, ...), custom_call_target="tpu_custom_call" | custom-call | tf_op jit(solution)/shard_map/pallas_call | solution.py:537
Async XLA Ops:
  0.6 63.2 %copy-start = (bf16[1,2,1024,1536]{3,2,1,0:T(8,128)(2,1)S(1)}, bf16[1,2,1024,1536]{3,2,1,0:T(8,128)(2,1)}, u32[]{:S(2)}) copy-start(bf16[1,2,1024,1536]{3,2,1,0:T(8,128)(2,1)} %param.3) | copy-start | bytes 18874372
  0.6 1.3 %copy-start.1 = (bf16[1,2,128,1536]{3,2,1,0:T(8,128)(2,1)S(1)}, bf16[1,2,128,1536]{3,2,1,0:T(8,128)(2,1)}, u32[]{:S(2)}) copy-start(bf16[1,2,128,1536]{3,2,1,0:T(8,128)(2,1)} %param.4) | copy-start | bytes 2359300
  1.9 0.9 %copy-start.2 = (s32[8,64]{1,0:T(8,128)S(1)}, s32[8,64]{1,0:T(8,128)}, u32[]{:S(2)}) copy-start(s32[8,64]{1,0:T(8,128)} %reach_ref.1) | copy-start | bytes 6148

commit v2 on v1

--- a/solution.py
+++ b/solution.py
@@ -119,7 +119,7 @@
 
 MESH = pl.DeviceIdType.MESH
 ROUND = 8
-EARLY_ROUNDS = 5
+EARLY_ROUNDS = 2
 
 
 def remote(src, dst, send_sem, recv_sem, device):
@@ -179,10 +179,11 @@
     groups,
     m_hbm,
     b_hbm,
-    reach_ref,
+    reach_hbm,
     q_ref,
     inv_ref,
     r_ref,
+    reach_ref,
     m_buf,
     b_buf,
     p_out,
@@ -197,6 +198,7 @@
     t_in,
     t_red,
     t_full,
+    reach_sem,
     m_sem,
     b_sem,
     p_send,
@@ -231,6 +233,7 @@
     def span(q):
         return pl.ds(pl.multiple_of(q * rows, rows), rows)
 
+    pltpu.make_async_copy(reach_hbm, reach_ref, reach_sem.at[0]).start()
     for k in range(2):
         pltpu.make_async_copy(b_hbm.at[k], b_buf.at[k], b_sem.at[k]).start()
     for o in order:
@@ -247,6 +250,7 @@
                 barrier, 1, device_id=(2 * zed + cc, lax.rem(sp + o, shards)), device_id_type=MESH
             )
 
+    pltpu.make_async_copy(reach_hbm, reach_ref, reach_sem.at[0]).wait()
     hot, cold = slot_classes(reach_ref[...].astype(jnp.float32), groups)
     mine = lax.broadcasted_iota(jnp.int32, (replicas, 1), 0) == me
     my_hot = jnp.sum(jnp.where(mine, hot, 0.0), axis=0, keepdims=True)
@@ -300,16 +304,6 @@
             q_out[i] = rounded
             g_out[zz, cc] = dot_tn(rounded, rounded).astype(jnp.bfloat16)
 
-        @pl.when(zz != zed)
-        def _():
-            remote(
-                g_out.at[zz], g_in.at[zed], g_send.at[zz], g_recv.at[zed], (2 * zz + core, sp)
-            ).start()
-
-        @pl.when(zz == zed)
-        def _():
-            g_in[zz] = g_out[zz]
-
     for o in range(1, replicas):
         dst = lax.rem(me + o, replicas)
         remote(
@@ -320,6 +314,49 @@
             (dst, sp),
         ).start()
     q_in[core, span(zed), :] = q_out[me]
+
+    for cc in range(2):
+        for zz in range(pieces):
+
+            @pl.when((cc != core) | (zz != zed))
+            def _():
+                remote(
+                    q_out.at[0],
+                    q_in.at[cc, pl.ds(zz * rows, rows)],
+                    q_send.at[0],
+                    q_recv.at[cc, zz],
+                    (2 * zz + cc, sp),
+                ).wait_recv()
+
+    for zz in range(pieces):
+
+        @pl.when(zz != zed)
+        def _():
+            remote(
+                g_out.at[zz], g_in.at[zed], g_send.at[zz], g_recv.at[zed], (2 * zz + core, sp)
+            ).start()
+
+        @pl.when(zz == zed)
+        def _():
+            g_in[zz] = g_out[zz]
+
+    for zz in range(pieces):
+        at = pl.ds(zz * rows, rows)
+        a = q_in[0, at, :].astype(jnp.float32)
+        b = q_in[1, at, :].astype(jnp.float32)
+        q_ref[0, at, :] = (a * first + b * (1.0 - first)).astype(jnp.bfloat16)
+        q_ref[1, at, :] = (b * first + a * (1.0 - first)).astype(jnp.bfloat16)
+    turned = [q_ref[k].T for k in range(2)]
+    for o in list(range(1, shards)) + [0]:
+        sq = lax.rem(sp + o, shards)
+        at = pl.ds(pl.multiple_of(sq * wide, wide), wide)
+        for k in range(2):
+            value = jnp.dot(turned[k], m_buf[k, :, at], preferred_element_type=jnp.float32)
+            t_out[o, k] = value.astype(jnp.bfloat16)
+        if o > 0:
+            remote(t_out.at[o], t_in.at[sp], t_send.at[o], t_recv.at[sp], (me, sq)).start()
+        else:
+            t_in[sp] = t_out[0]
 
     for o in range(1, pieces):
         src = piece_at(o)
@@ -362,39 +399,6 @@
     rounds = rank // ROUND
     mat = lax.fori_loop(0, EARLY_ROUNDS, eliminate_round, mat)
 
-    for cc in range(2):
-        for zz in range(pieces):
-
-            @pl.when((cc != core) | (zz != zed))
-            def _():
-                remote(
-                    q_out.at[0],
-                    q_in.at[cc, pl.ds(zz * rows, rows)],
-                    q_send.at[0],
-                    q_recv.at[cc, zz],
-                    (2 * zz + cc, sp),
-                ).wait_recv()
-
-    for zz in range(pieces):
-        at = pl.ds(zz * rows, rows)
-        a = q_in[0, at, :].astype(jnp.float32)
-        b = q_in[1, at, :].astype(jnp.float32)
-        q_ref[0, at, :] = (a * first + b * (1.0 - first)).astype(jnp.bfloat16)
-        q_ref[1, at, :] = (b * first + a * (1.0 - first)).astype(jnp.bfloat16)
-    turned = [q_ref[k].T for k in range(2)]
-    for o in list(range(1, shards)) + [0]:
-        sq = lax.rem(sp + o, shards)
-        at = pl.ds(pl.multiple_of(sq * wide, wide), wide)
-        for k in range(2):
-            value = jnp.dot(turned[k], m_buf[k, :, at], preferred_element_type=jnp.float32)
-            t_out[o, k] = value.astype(jnp.bfloat16)
-        if o > 0:
-            remote(t_out.at[o], t_in.at[sp], t_send.at[o], t_recv.at[sp], (me, sq)).start()
-        else:
-            t_in[sp] = t_out[0]
-
-    mat = lax.fori_loop(EARLY_ROUNDS, rounds, eliminate_round, mat)
-
     for o in range(1, shards):
         sq = lax.rem(sp + o, shards)
         remote(t_out.at[0], t_in.at[sq], t_send.at[0], t_recv.at[sq], (me, sq)).wait_recv()
@@ -407,6 +411,7 @@
         sq = lax.rem(sp + o, shards)
         remote(t_red, t_full.at[sp], f_send.at[o], f_recv.at[sp], (me, sq)).start()
     t_full[sp] = t_red[...]
+    mat = lax.fori_loop(EARLY_ROUNDS, rounds, eliminate_round, mat)
 
     below = lax.broadcasted_iota(jnp.int32, square, 0) > lax.broadcasted_iota(jnp.int32, square, 1)
     inverse = []
@@ -489,7 +494,7 @@
     bf16 = jnp.bfloat16
     dma = pltpu.SemaphoreType.DMA
     vmem = pl.BlockSpec(memory_space=pltpu.VMEM)
-    hbm = pl.BlockSpec(memory_space=pl.ANY)
+    hbm = pl.BlockSpec(memory_space=pltpu.HBM)
     q, inv, r = pl.pallas_call(
         functools.partial(power_kernel, NGROUP),
         out_shape=(
@@ -497,9 +502,10 @@
             jax.ShapeDtypeStruct((2, rank, rank), bf16),
             jax.ShapeDtypeStruct((2, rank, cols), bf16),
         ),
-        in_specs=[hbm, hbm, vmem],
+        in_specs=[hbm, hbm, hbm],
         out_specs=(vmem, vmem, vmem),
         scratch_shapes=[
+            pltpu.VMEM(reach_map.shape, jnp.int32),
             pltpu.VMEM((2, rows_dev, cols), bf16),
             pltpu.VMEM((2, rank, cols), bf16),
             pltpu.VMEM((pieces, 2, rows, rank), bf16),
@@ -514,6 +520,7 @@
             pltpu.VMEM((shards, 2, rank, wide), bf16),
             pltpu.VMEM((2, rank, wide), bf16),
             pltpu.VMEM((shards, 2, rank, wide), bf16),
+            dma((1,)),
             dma((pieces, 2)),
             dma((2,)),
             dma((pieces, 2)),

time: 69.3 us -> 65.5 us (0.945)
  the two profiles are of different devices: /device:TPU:0 before, /device:TPU:24 now
where the time goes in v2:
time: 65.5 us; the launch traced here: 65.3 us
  Pallas kernels  62.4 us (95%)
  local copies, waits for them, and re-layouts  2.21 us (3%)
  between operations  0.66 us (1%)
    pallas_call x1, Pallas kernels, fused_on_device(): pl.pallas_call(functools.partial(power_kernel, NGROUP), out_shape=(jax.Sh...  57.2 us
    pallas_call x1, Pallas kernels, fused_on_device(): pl.pallas_call(functools.partial(finish_kernel, rows_dev * shards), grid=...  5.21 us
    unnamed x6, local copies, waits for them, and re-layouts  2.21 us

profile of v2, /device:TPU:24, one launch (start us, length us, event | category | flops | bytes accessed | tf_op | source)
XLA Modules:
  0.0 65.3 jit_solution(972336317519296295)
XLA Ops:
  0.6 0.0 copy-start
  0.6 0.0 copy-start.1
  0.7 1.3 %copy-done.1 = bf16[1,2,128,1536]{3,2,1,0:T(8,128)(2,1)S(1)} copy-done((bf16[1,2,128,1536]{3,2,1,0:T(8,128)(2,1)S(1)}, bf16[1,2,128,1536]{3,2,1,0:T(8,128)(2,1)}, u32[]{:S(2)}) %copy-start.1) | copy-done | bytes 786456
  1.9 0.0 copy-start.2
  1.9 0.9 %copy-done.2 = s32[8,64]{1,0:T(8,128)S(1)} copy-done((s32[8,64]{1,0:T(8,128)S(1)}, s32[8,64]{1,0:T(8,128)}, u32[]{:S(2)}) %copy-start.2) | copy-done | bytes 2072
  2.9 57.2 %shard_map.58 = (bf16[2,1024,128]{2,1,0:T(8,128)(2,1)S(1)}, bf16[2,128,128]{2,1,0:T(8,128)(2,1)S(1)}, bf16[2,128,1536]{2,1,0:T(8,128)(2,1)S(1)}) custom-call(bf16[2,1024,1536]{2,1,0:T(8,128)(2,1)} %bitcast.5, bf16[2,128,1536]{2,1,0:T(8,128)(2,1)S(1)} %bitcast.7, s32[8,64]{1,0:T(8,128)S(1)} %copy-done.2), custom_call_target="tpu_custom_call" | custom-call | tf_op jit(solution)/shard_map/pallas_call | solution.py:498
  60.1 0.0 copy-done
  60.1 5.2 %shard_map.59 = (bf16[2,1024,1536]{2,1,0:T(8,128)(2,1)}, bf16[2,128,1536]{2,1,0:T(8,128)(2,1)}, bf16[2,1024,128]{2,1,0:T(8,128)(2,1)}) custom-call(bf16[2,1024,1536]{2,1,0:T(8,128)(2,1)S(1)} %bitcast.6, bf16[2,1024,128]{2,1,0:T(8,128)(2,1)S(1)} %get-tuple-element.9.q_ref, bf16[2,128,128]{2,1,0:T(8,128)(2,1)S(1)} %get-tuple-element.10.inv_ref, ...), custom_call_target="tpu_custom_call" | custom-call | tf_op jit(solution)/shard_map/pallas_call | solution.py:544
Async XLA Ops:
  0.6 59.4 %copy-start = (bf16[1,2,1024,1536]{3,2,1,0:T(8,128)(2,1)S(1)}, bf16[1,2,1024,1536]{3,2,1,0:T(8,128)(2,1)}, u32[]{:S(2)}) copy-start(bf16[1,2,1024,1536]{3,2,1,0:T(8,128)(2,1)} %param.3) | copy-start | bytes 18874372
  0.6 1.3 %copy-start.1 = (bf16[1,2,128,1536]{3,2,1,0:T(8,128)(2,1)S(1)}, bf16[1,2,128,1536]{3,2,1,0:T(8,128)(2,1)}, u32[]{:S(2)}) copy-start(bf16[1,2,128,1536]{3,2,1,0:T(8,128)(2,1)} %param.4) | copy-start | bytes 2359300
  1.9 0.9 %copy-start.2 = (s32[8,64]{1,0:T(8,128)S(1)}, s32[8,64]{1,0:T(8,128)}, u32[]{:S(2)}) copy-start(s32[8,64]{1,0:T(8,128)} %reach_hbm.1) | copy-start | bytes 6148

commit v3 on v2

--- a/solution.py
+++ b/solution.py
@@ -119,7 +119,7 @@
 
 MESH = pl.DeviceIdType.MESH
 ROUND = 8
-EARLY_ROUNDS = 2
+EARLY_ROUNDS = 0
 
 
 def remote(src, dst, send_sem, recv_sem, device):

time: 65.5 us -> 65.5 us (level)
  no operation moved by 1% of the time
where the time goes in v3:
time: 65.5 us; the launch traced here: 65.3 us
  Pallas kernels  62.4 us (95%)
  local copies, waits for them, and re-layouts  2.21 us (3%)
  between operations  0.66 us (1%)
    pallas_call x1, Pallas kernels, fused_on_device(): pl.pallas_call(functools.partial(power_kernel, NGROUP), out_shape=(jax.Sh...  57.2 us
    pallas_call x1, Pallas kernels, fused_on_device(): pl.pallas_call(functools.partial(finish_kernel, rows_dev * shards), grid=...  5.21 us
    unnamed x6, local copies, waits for them, and re-layouts  2.21 us

profile of v3, /device:TPU:24, one launch (start us, length us, event | category | flops | bytes accessed | tf_op | source)
XLA Modules:
  0.0 65.3 jit_solution(2327432342402625968)
XLA Ops:
  0.6 0.0 copy-start
  0.6 0.0 copy-start.1
  0.7 1.3 %copy-done.1 = bf16[1,2,128,1536]{3,2,1,0:T(8,128)(2,1)S(1)} copy-done((bf16[1,2,128,1536]{3,2,1,0:T(8,128)(2,1)S(1)}, bf16[1,2,128,1536]{3,2,1,0:T(8,128)(2,1)}, u32[]{:S(2)}) %copy-start.1) | copy-done | bytes 786456
  1.9 0.0 copy-start.2
  1.9 0.9 %copy-done.2 = s32[8,64]{1,0:T(8,128)S(1)} copy-done((s32[8,64]{1,0:T(8,128)S(1)}, s32[8,64]{1,0:T(8,128)}, u32[]{:S(2)}) %copy-start.2) | copy-done | bytes 2072
  2.9 57.2 %shard_map.58 = (bf16[2,1024,128]{2,1,0:T(8,128)(2,1)S(1)}, bf16[2,128,128]{2,1,0:T(8,128)(2,1)S(1)}, bf16[2,128,1536]{2,1,0:T(8,128)(2,1)S(1)}) custom-call(bf16[2,1024,1536]{2,1,0:T(8,128)(2,1)} %bitcast.5, bf16[2,128,1536]{2,1,0:T(8,128)(2,1)S(1)} %bitcast.7, s32[8,64]{1,0:T(8,128)S(1)} %copy-done.2), custom_call_target="tpu_custom_call" | custom-call | tf_op jit(solution)/shard_map/pallas_call | solution.py:498
  60.1 0.0 copy-done
  60.1 5.2 %shard_map.59 = (bf16[2,1024,1536]{2,1,0:T(8,128)(2,1)}, bf16[2,128,1536]{2,1,0:T(8,128)(2,1)}, bf16[2,1024,128]{2,1,0:T(8,128)(2,1)}) custom-call(bf16[2,1024,1536]{2,1,0:T(8,128)(2,1)S(1)} %bitcast.6, bf16[2,1024,128]{2,1,0:T(8,128)(2,1)S(1)} %get-tuple-element.9.q_ref, bf16[2,128,128]{2,1,0:T(8,128)(2,1)S(1)} %get-tuple-element.10.inv_ref, ...), custom_call_target="tpu_custom_call" | custom-call | tf_op jit(solution)/shard_map/pallas_call | solution.py:544
Async XLA Ops:
  0.6 59.5 %copy-start = (bf16[1,2,1024,1536]{3,2,1,0:T(8,128)(2,1)S(1)}, bf16[1,2,1024,1536]{3,2,1,0:T(8,128)(2,1)}, u32[]{:S(2)}) copy-start(bf16[1,2,1024,1536]{3,2,1,0:T(8,128)(2,1)} %param.3) | copy-start | bytes 18874372
  0.6 1.3 %copy-start.1 = (bf16[1,2,128,1536]{3,2,1,0:T(8,128)(2,1)S(1)}, bf16[1,2,128,1536]{3,2,1,0:T(8,128)(2,1)}, u32[]{:S(2)}) copy-start(bf16[1,2,128,1536]{3,2,1,0:T(8,128)(2,1)} %param.4) | copy-start | bytes 2359300
  1.9 0.9 %copy-start.2 = (s32[8,64]{1,0:T(8,128)S(1)}, s32[8,64]{1,0:T(8,128)}, u32[]{:S(2)}) copy-start(s32[8,64]{1,0:T(8,128)} %reach_hbm.1) | copy-start | bytes 6148
